TPU v7x, 256 devices: a whole 4x4x8 slice. The times are simulated.
256 devices in a mesh: outer: 32 (over z, x_lo, core), inner: 8 (over y, x_hi).
Axes of the slice: x: 4 (x_hi: 2, x_lo: 2; x = x_hi * 2 + x_lo), y: 4, z: 8, core: 2. Of those that a mesh axis runs over, the one named last changes fastest.
Arguments:
- query: bfloat16 [131072, 512], P(('outer', 'inner')), may hold values from -28 to 28
- keys: bfloat16 [131072, 512], P(('outer', 'inner')), may hold values from -28 to 28
- values: bfloat16 [131072, 512], P(('outer', 'inner')), may hold values from -6 to 6
- grad_out: bfloat16 [131072, 512], P(('outer', 'inner')), may hold values from -30 to 30
- band: int32 [512, 5], P(('outer', 'inner')), may hold values from -1 to 511, as said below
- prefix_len: int32 [1], replicated, may hold values from 256 to 512
Outputs:
- attended: bfloat16 [131072, 512], P(('outer', 'inner'))
- grad_query: bfloat16 [131072, 512], P(('outer', 'inner'))
- grad_keys: bfloat16 [131072, 512], P(('outer', 'inner'))
- grad_values: bfloat16 [131072, 512], P(('outer', 'inner'))
Inputs may be any that keep to these rules, and one draw needn't show every extreme that they name: `band`: row b lists in slot s either block b - 2 + s or -1; the listed blocks form a run that always holds b itself, with lengths of the run before and after b drawn independently from 0 to 2.
All inputs are finite; a program needn't handle non-finite values.
Results may differ from a plain program's by a relative error of at most 0.025.
Values may be sent and summed in bfloat16 or wider, within the bound.
A program may use at most 128 MiB of HBM per device.

v0:
```python
import jax
import jax.numpy as jnp
from jax import lax
from jax.sharding import PartitionSpec as P

HEADS = 8
HEAD = 64
PRE = 512
BLK = 256


def shifted(shard, axis, by):
    peers = lax.axis_size(axis)
    pairs = [(i, i + by) for i in range(peers) if 0 <= i + by < peers]
    return lax.ppermute(shard, axis, pairs)


def spread(value, axis, source):
    kept = jnp.where(lax.axis_index(axis) == source, value, 0).astype(value.dtype)
    return lax.psum(kept, axis)


def allowed_mask(band_rows, device, prefix_len, rows, block):
    per = rows // block
    kblock = (device - 1) * per + jnp.arange(3 * per, dtype=jnp.int32)
    match = jnp.any(band_rows[:, :, None] == kblock[None, None, :], axis=1) & (kblock >= 0)[None, :]
    grid = jnp.repeat(jnp.repeat(match, block, axis=0), block, axis=1)
    frame = (device - 1) * rows + jnp.arange(3 * rows, dtype=jnp.int32)
    grid = grid & (frame >= prefix_len[0])[None, :]
    prompt = jnp.arange(PRE, dtype=jnp.int32) < prefix_len[0]
    prompt = jnp.broadcast_to(prompt[None, :], (rows, PRE))
    return jnp.concatenate([grid, prompt], axis=1)


def attend_pair(query, cand_k, cand_v, grad_out, allowed):
    scale = HEAD ** (-0.5)
    scores = jnp.einsum("qhd,khd->hqk", query, cand_k, preferred_element_type=jnp.float32) * scale
    scores = jnp.where(allowed[None], scores, -jnp.inf)
    top = jnp.max(scores, axis=-1, keepdims=True)
    expo = jnp.exp(scores - top)
    probs = expo / jnp.sum(expo, axis=-1, keepdims=True)
    probs_b = probs.astype(jnp.bfloat16)
    attended = jnp.einsum(
        "hqk,khd->qhd", probs_b, cand_v, preferred_element_type=jnp.float32
    ).astype(jnp.bfloat16)
    dprobs = jnp.einsum("qhd,khd->hqk", grad_out, cand_v, preferred_element_type=jnp.float32)
    delta = jnp.sum(probs * dprobs, axis=-1, keepdims=True)
    dscores = (probs * (dprobs - delta)).astype(jnp.bfloat16)
    grad_query = (
        jnp.einsum("hqk,khd->qhd", dscores, cand_k, preferred_element_type=jnp.float32) * scale
    ).astype(jnp.bfloat16)
    grad_keys = (
        jnp.einsum("hqk,qhd->khd", dscores, query, preferred_element_type=jnp.float32) * scale
    )
    grad_values = jnp.einsum("hqk,qhd->khd", probs_b, grad_out, preferred_element_type=jnp.float32)
    return (attended, grad_query, grad_keys, grad_values)


def on_device(query, keys, values, grad_out, band, prefix_len):
    rows = query.shape[0]
    width = query.shape[1]
    pairs = HEADS // 2
    device = lax.axis_index(("outer", "inner"))
    stacked = jnp.stack([keys, values])
    found = []
    for step_by in (1, -1):
        found.append(shifted(stacked, ("outer", "inner"), step_by))
    near = jnp.concatenate([found[0], stacked, found[1]], axis=1)
    prompt = spread(stacked, ("outer", "inner"), 0)
    cand = jnp.concatenate([near, prompt], axis=1)
    allowed = allowed_mask(band, device, prefix_len, rows, BLK)

    def split_heads(array):
        return jnp.moveaxis(array.reshape(array.shape[0], pairs, 2, HEAD), 1, 0)

    def join_heads(array):
        return jnp.moveaxis(array, 0, 1).reshape(array.shape[1], width)

    def per_pair(items):
        return attend_pair(items[0], items[1], items[2], items[3], allowed)

    results = lax.map(
        per_pair,
        (split_heads(query), split_heads(cand[0]), split_heads(cand[1]), split_heads(grad_out)),
    )
    attended = join_heads(results[0])
    grad_query = join_heads(results[1])
    parts = jnp.stack([join_heads(results[2]), join_heads(results[3])])
    band_parts = parts[:, : 3 * rows].astype(jnp.bfloat16)
    returned = []
    for step_by in (-1, 1):
        piece = band_parts[:, :rows] if step_by == -1 else band_parts[:, 2 * rows :]
        returned.append(shifted(piece, ("outer", "inner"), step_by))
    total = (
        band_parts[:, rows : 2 * rows].astype(jnp.float32)
        + returned[1].astype(jnp.float32)
        + returned[0].astype(jnp.float32)
    )
    prompt_parts = parts[:, 3 * rows :]
    summed = lax.psum(prompt_parts, ("outer", "inner"))
    total = total + jnp.where(device == 0, summed, jnp.zeros_like(summed))
    return (attended, grad_query, total[0].astype(jnp.bfloat16), total[1].astype(jnp.bfloat16))


def solution(mesh):
    placed = (
        P(("outer", "inner"), None),
        P(("outer", "inner"), None),
        P(("outer", "inner"), None),
        P(("outer", "inner"), None),
        P(("outer", "inner"), None),
        P(),
    )
    return jax.shard_map(
        on_device,
        mesh=mesh,
        in_specs=placed,
        out_specs=(
            P(("outer", "inner"), None),
            P(("outer", "inner"), None),
            P(("outer", "inner"), None),
            P(("outer", "inner"), None),
        ),
        check_vma=False,
    )
```

profile of v0, /device:TPU:0, one launch (start us, length us, event | category | flops | bytes accessed | tf_op | source)
XLA Modules:
  0.0 707.5 jit_solution(1830515460373131769)
XLA Ops:
  11.2 4.2 collective-permute-start
  19.1 2.9 copy.40
  23.5 271.1 %all-reduce.3.cloned.1.call-done = bf16[2,512,512]{1,2,0:T(8,128)(2,1)} async-done(((bf16[2,512,512]{1,2,0:T(8,128)(2,1)}), bf16[2,512,512]{1,2,0:T(8,128)(2,1)}) %all-reduce.3.cloned.1.call-update) | async-done | bytes 1048592 | tf_op jit(solution)/shard_map/psum | solution.py:20
  294.6 2.1 pad_maximum_fusion.1
  298.5 90.4 %while.16 = (s32[]{:T(128)}, bf16[4,512,2,64]{1,3,2,0:T(8,128)(2,1)}, bf16[4,512,2,64]{1,3,2,0:T(8,128)(2,1)}, f32[4,2048,2,64]{1,3,2,0:T(8,128)}, f32[4,2048,2,...) while((s32[]{:T(128)}, ...), condition=%wide.region_6.7_spmd, body=%wide.region_2.6_spmd.sunk | while | flops 1642529792 | bytes 136087792 | solution.py:82
  298.5 6.2 fusion.108
  304.7 4.6 multiply_reduce_fusion.2
  317.9 3.2 fusion.109
  321.1 6.2 fusion.108
  327.3 4.6 multiply_reduce_fusion.2
  336.5 2.1 fusion.110
  340.5 3.2 fusion.109
  343.7 6.2 fusion.108
  349.9 4.6 multiply_reduce_fusion.2
  363.1 3.2 fusion.109
  366.3 6.2 fusion.108
  372.5 4.6 multiply_reduce_fusion.2
  385.6 3.2 fusion.109
  388.8 6.2 fusion.68
  395.1 2.8 fusion.69
  397.9 2.8 fusion.79
  400.7 5.0 collective-permute-start.2
  411.1 285.0 %all-reduce.5.cloned.1.call-done = f32[2,512,512]{1,2,0:T(8,128)} async-done(((f32[2,512,512]{1,2,0:T(8,128)}), f32[2,512,512]{1,2,0:T(8,128)}) %all-reduce.5.cloned.1.call-update) | async-done | bytes 2097168 | tf_op jit(solution)/shard_map/psum | solution.py:100
  696.1 2.5 add_convert_fusion
  (92 shorter events, 49.7 us)
Async XLA Ops:
  7.2 10.3 %copy-start.4 = (s32[2,5]{1,0:T(2,128)S(1)}, s32[2,5]{1,0:T(2,128)}, u32[]{:S(2)}) copy-start(s32[2,5]{1,0:T(2,128)} %param.12) | copy-start | bytes 124
  7.2 287.4 %all-reduce.3.cloned.1.call-start = ((), (), s32[]{:S(2)}) async-start(), calls=%async_computation | async-start | bytes 2097152 | tf_op jit(solution)/shard_map/psum | solution.py:20
  9.8 12.3 %copy-start.3 = (bf16[512,512]{1,0:T(8,128)(2,1)S(1)}, bf16[512,512]{1,0:T(8,128)(2,1)}, u32[]{:S(2)}) copy-start(bf16[512,512]{1,0:T(8,128)(2,1)} %param.8) | copy-start | bytes 1572868
  11.2 283.3 %collective-permute-start = (bf16[2,512,512]{1,2,0:T(8,128)(2,1)}, bf16[2,512,512]{1,2,0:T(8,128)(2,1)}, u32[]{:S(2)}, u32[]{:S(2)}) collective-permute-start(bf16[2,512,512]{1,2,0:T(8,128)(2,1)} %get-tuple-element.135), channel_id=1, source_target_pairs={{0,1},{1,2},{2,3},{3,4},{4,5},{5,6},{6,7},{7,8},{8,9},{9,10},{10,1... | collective-permute-start | bytes 3145736 | tf_op jit(solution)/shard_map/ppermute | solution.py:15
  15.4 279.2 %collective-permute-start.1 = (bf16[2,512,512]{1,2,0:T(8,128)(2,1)}, bf16[2,512,512]{1,2,0:T(8,128)(2,1)}, u32[]{:S(2)}, u32[]{:S(2)}) collective-permute-start(bf16[2,512,512]{1,2,0:T(8,128)(2,1)} %get-tuple-element.135), channel_id=1, source_target_pairs={{1,0},{2,1},{3,2},{4,3},{5,4},{6,5},{7,6},{8,7},{9,8},{10,9},{11,1... | collective-permute-start | bytes 3145736 | tf_op jit(solution)/shard_map/ppermute | solution.py:15
  16.7 679.4 %all-reduce.5.cloned.1.call-start = ((), (), s32[]{:S(2)}) async-start(), calls=%async_computation.1 | async-start | bytes 4194304 | tf_op jit(solution)/shard_map/psum | solution.py:100
  304.7 4.8 slice-start
  304.7 6.1 slice-start.1
  310.8 2.2 copy-start
  313.8 4.1 copy-start.1
  327.3 4.8 slice-start
  327.3 6.1 slice-start.1
  333.4 2.2 copy-start
  336.4 4.0 copy-start.1
  349.9 4.8 slice-start
  349.9 6.1 slice-start.1
  359.0 4.0 copy-start.1
  372.5 4.8 slice-start
  372.5 6.1 slice-start.1
  378.6 2.2 copy-start
  381.6 4.0 copy-start.1
  388.8 6.2 copy-start.2
  400.7 295.4 %collective-permute-start.2 = (bf16[2,512,512]{1,2,0:T(8,128)(2,1)}, bf16[2,512,512]{1,2,0:T(8,128)(2,1)S(1)}, u32[]{:S(2)}, u32[]{:S(2)}) collective-permute-start(bf16[2,512,512]{1,2,0:T(8,128)(2,1)} %get-tuple-element.129), channel_id=1, source_target_pairs={{0,1},{1,2},{2,3},{3,4},{4,5},{5,6},{6,7},{7,8},{8,9},{9,10},{10,1... | collective-permute-start | bytes 3145736 | tf_op jit(solution)/shard_map/ppermute | solution.py:15
  405.7 290.4 %collective-permute-start.3 = (bf16[2,512,512]{1,2,0:T(8,128)(2,1)S(1)}, bf16[2,512,512]{1,2,0:T(8,128)(2,1)S(1)}, u32[]{:S(2)}, u32[]{:S(2)}) collective-permute-start(bf16[2,512,512]{1,2,0:T(8,128)(2,1)S(1)} %get-tuple-element.130), channel_id=1, source_target_pairs={{1,0},{2,1},{3,2},{4,3},{5,4},{6,5},{7,6},{8,7},{9,8},{10,9},{11,1... | collective-permute-start | bytes 3145736 | tf_op jit(solution)/shard_map/ppermute | solution.py:15
  (1 other events, 2.2 us)
Sparse Core Ops, SparseCore 0:
  16.8 277.6 all-reduce.2
  405.9 290.2 all-reduce.4
where the time goes:
time: 710 us; the launch traced here: 708 us
  waiting for transfers between devices  556 us (78%)
  matrix products  75.7 us (11%)
  local copies, waits for them, and re-layouts  26.8 us (4%)
  other arithmetic  22 us (3%)
  between operations  14.9 us (2%)
  starting transfers between devices  11.8 us (2%)
    psum x1, waiting for transfers between devices, on_device(): summed = lax.psum(prompt_parts, ('outer', 'inner'))  285 us
    psum x1, waiting for transfers between devices, spread(): return lax.psum(kept, axis)  271 us
    sub x4, matrix products, attend_pair(): expo = jnp.exp(scores - top)  24.8 us
    dot_general x4, matrix products, attend_pair(): jnp.einsum('qhd,khd->hqk', grad_out, cand_v, preferred_element_type=jnp.f...  18.5 us
  transfers between devices with their start and end apart: 6, of which 2 were waited for; matrix products, arithmetic and copies ran while one was open for 1% of the time, Pallas kernels for 0%

commit v1 on v0

v1 whole, which is shorter than its diff:
```python
import functools

import jax
import jax.numpy as jnp
from jax import lax
from jax.experimental import pallas as pl
from jax.experimental.pallas import tpu as pltpu
from jax.sharding import PartitionSpec as P

F32 = jnp.float32
BF = jnp.bfloat16
MESH = pl.DeviceIdType.MESH
BLK = 256
ROWS = 512
WIDTH = 512
PAIR = 128
PAIRS = 4
HEAD = 64
SLOTS = 5
TILES = 7
KEYS = TILES * BLK
CAND = 2048
SCALE = HEAD ** -0.5
TO_EXP2 = SCALE * 1.4426950408889634
OFF = -1e30
PLANE = 16
PIECE = 32


def dot_last(a, b):
    return lax.dot_general(a, b, (((1,), (1,)), ((), ())), preferred_element_type=F32)


def dot(a, b):
    return lax.dot_general(a, b, (((1,), (0,)), ((), ())), preferred_element_type=F32)


def tile_rows(qb, s):
    low = (qb + s) * BLK if s < SLOTS else 3 * ROWS + (s - SLOTS) * BLK
    return slice(low, low + BLK)


def fill_bias(band, plen, bias, device):
    row = lax.broadcasted_iota(jnp.int32, (BLK, PAIR), 0)
    for qb in range(2):
        for s in range(SLOTS):
            block = 2 * device + qb - 2 + s
            ok = (block * BLK + row >= plen[0]) & (band[qb, s] >= 0)
            bias[qb, s * BLK : (s + 1) * BLK, :] = jnp.where(ok, 0.0, OFF)
        for s in range(2):
            low = (SLOTS + s) * BLK
            bias[qb, low : low + BLK, :] = jnp.where(row + s * BLK < plen[0], 0.0, OFF)


def attend_pair(p, q, g, kv, bias, kt, vt, gt, x, e, dk, dv, att_t, dq_t, att, dq):
    cols = pl.ds(pl.multiple_of(p * PAIR, PAIR), PAIR)
    lane = lax.broadcasted_iota(jnp.int32, (BLK, PAIR), 1)
    kt[...] = kv[0, :, cols].T
    vt[...] = kv[1, :, cols].T
    gt[...] = g[:, cols].T
    dk[...] = jnp.zeros_like(dk)
    dv[...] = jnp.zeros_like(dv)
    for qb in range(2):
        mine = slice(qb * BLK, (qb + 1) * BLK)
        for h in range(2):
            half = (lane < HEAD) if h == 0 else (lane >= HEAD)
            heads = slice(h * HEAD, (h + 1) * HEAD)
            qz = jnp.where(half, q[mine, cols], jnp.zeros((), BF))
            top = jnp.full((8, BLK), OFF, F32)
            for s in range(TILES):
                t = dot_last(kv[0, tile_rows(qb, s), cols], qz) * TO_EXP2
                b = bias[qb, s * BLK : (s + 1) * BLK, :]
                t = t + jnp.concatenate([b, b], axis=1)
                x[s * BLK : (s + 1) * BLK, :] = t
                top = jnp.maximum(top, jnp.max(t.reshape(BLK // 8, 8, BLK), axis=0))
            top = jnp.max(top, axis=0, keepdims=True)
            total = jnp.zeros((8, BLK), F32)
            a = jnp.zeros((HEAD, BLK), F32)
            for s in range(TILES):
                expo = jnp.exp2(x[s * BLK : (s + 1) * BLK, :] - top)
                total = total + jnp.sum(expo.reshape(BLK // 8, 8, BLK), axis=0)
                eb = expo.astype(BF)
                e[s * BLK : (s + 1) * BLK, :] = eb
                a = a + dot(vt[heads, tile_rows(qb, s)], eb)
            r = 1.0 / jnp.sum(total, axis=0, keepdims=True)
            a = a * r
            att_t[heads, :] = a
            r_col = jnp.broadcast_to(r, (PAIR, BLK)).T
            gz = jnp.where(half, g[mine, cols].astype(F32) * r_col, 0.0).astype(BF)
            g_row = (gt[heads, mine].astype(F32) * r).astype(BF).astype(F32)
            delta = jnp.sum(g_row * a, axis=0, keepdims=True)
            d = jnp.zeros((HEAD, BLK), F32)
            for s in range(TILES):
                rows = tile_rows(qb, s)
                eb = e[s * BLK : (s + 1) * BLK, :]
                dp = dot_last(kv[1, rows, cols], gz) - delta
                ds = (eb.astype(F32) * dp).astype(BF)
                dv[rows, :] += dot(eb, gz)
                dk[rows, :] += dot(ds, qz)
                d = d + dot(kt[heads, rows], ds)
            dq_t[heads, :] = d * SCALE
        att[mine, cols] = att_t[...].T.astype(BF)
        dq[mine, cols] = dq_t[...].T.astype(BF)


def wait_bytes(ref, sem):
    pltpu.make_async_copy(ref, ref, sem).wait()


def kernel(
    band, plen, q, k, v, g, att, dq, out_k, out_v,
    kv, bias, kt, vt, gt, x, e, dk, dv, att_t, dq_t,
    own, ys, yr, xs, xr, ps, pr, rb, rc, pz, rz, pf, rf,
    local_sem, hx_s, hx_r, hy_s, hy_r, b1_s, b1_r, b2_s, b2_r, b3_s, b3_r, b4_s, b4_r,
    y_s, y_r, x_s, x_r, r1_s, r1_r, r2_s, r2_r, r3_s, r3_r, r4_s, r4_r,
):
    outer = lax.axis_index("outer")
    inner = lax.axis_index("inner")
    device = outer * 8 + inner
    z = outer // 4
    x_lo = (outer // 2) % 2
    core = outer % 2
    spot = x_lo * 8 + inner
    odd = inner % 2
    partner = (outer, inner + 1 - 2 * odd)
    ahead = lax.rem(device + 2 - 4 * odd + 256, 256)
    behind = lax.rem(device - 2 + 4 * odd + 256, 256)
    ahead = (ahead // 8, ahead % 8)
    behind = (behind // 8, behind % 8)
    other_core = (outer + 1 - 2 * core, inner)
    root = (0, 0)
    first = device == 0
    bottom = z == 0

    def in_plane(level, at, which):
        return ((level * 2 + at // 8) * 2 + which, at % 8)

    def in_column(level):
        return ((level * 2 + x_lo) * 2 + core, inner)

    def plane_peer(n):
        return lax.rem(spot + 1 + n, PLANE)

    def root_peer(n):
        return in_plane(0, n % PLANE, n // PLANE)

    mine_in = [
        pltpu.make_async_copy(k, kv.at[0, pl.ds(ROWS, ROWS)], local_sem.at[0]),
        pltpu.make_async_copy(v, kv.at[1, pl.ds(ROWS, ROWS)], local_sem.at[1]),
    ]
    for c in mine_in:
        c.start()

    barrier = pltpu.get_barrier_semaphore()

    def hello(target):
        pl.semaphore_signal(barrier, inc=1, device_id=target, device_id_type=MESH)

    for target in (partner, ahead, behind, other_core):
        hello(target)

    @pl.loop(0, PLANE - 1)
    def _(n):
        hello(in_plane(z, plane_peer(n), core))

    @pl.when(bottom)
    def _():
        @pl.loop(1, 8)
        def _(n):
            hello(in_column(n))

    @pl.when(jnp.logical_not(bottom))
    def _():
        hello(in_column(0))

    @pl.when(first)
    def _():
        @pl.loop(1, 2 * PLANE)
        def _(n):
            hello(root_peer(n))

    @pl.when(jnp.logical_and(bottom, jnp.logical_not(first)))
    def _():
        hello(root)

    for c in mine_in:
        c.wait()
    greeted = 4 + PLANE - 1 + jnp.where(bottom, 7, 1)
    greeted = greeted + jnp.where(first, 2 * PLANE - 1, jnp.where(bottom, 1, 0))
    pl.semaphore_wait(barrier, greeted)

    def send(src, dst, s_sem, r_sem, target):
        return pltpu.make_async_remote_copy(
            src_ref=src, dst_ref=dst, send_sem=s_sem, recv_sem=r_sem,
            device_id=target, device_id_type=MESH,
        )

    far = pl.multiple_of(odd * 1024, ROWS)
    near = pl.multiple_of((1 - odd) * 1024, ROWS)

    def columns(c):
        return pl.ds(pl.multiple_of(c * PAIR, PAIR), PAIR)

    def halo_x(c):
        return send(
            kv.at[:, pl.ds(ROWS, ROWS), columns(c)], kv.at[:, pl.ds(far, ROWS), columns(c)],
            hx_s.at[c], hx_r.at[c], partner,
        )

    def halo_y(c):
        return send(
            kv.at[:, pl.ds(near, ROWS), columns(c)], kv.at[:, pl.ds(far, ROWS), columns(c)],
            hy_s.at[c], hy_r.at[c], ahead,
        )

    def piece(at):
        return kv.at[core, pl.ds(pl.multiple_of(3 * ROWS + at * PIECE, PIECE), PIECE)]

    @pl.when(first)
    def _():
        @pl.loop(1, 2 * PLANE)
        def _(n):
            at = n % PLANE
            which = n // PLANE
            send(
                kv.at[which, pl.ds(pl.multiple_of(ROWS + at * PIECE, PIECE), PIECE)],
                kv.at[which, pl.ds(pl.multiple_of(3 * ROWS + at * PIECE, PIECE), PIECE)],
                b1_s, b1_r, root_peer(n),
            ).start()

        own_piece = pltpu.make_async_copy(
            kv.at[0, pl.ds(ROWS, PIECE)], kv.at[0, pl.ds(3 * ROWS, PIECE)], local_sem.at[0]
        )
        own_piece.start()
        own_piece.wait()

    @pl.loop(0, PAIRS)
    def _(c):
        halo_x(c).start()

    fill_bias(band, plen, bias, device)

    @pl.when(jnp.logical_and(bottom, jnp.logical_not(first)))
    def _():
        wait_bytes(piece(spot), b1_r)

    @pl.when(bottom)
    def _():
        @pl.loop(1, 8)
        def _(n):
            send(piece(spot), piece(spot), b2_s, b2_r, in_column(n)).start()

    @pl.when(jnp.logical_not(bottom))
    def _():
        wait_bytes(piece(spot), b2_r)

    @pl.loop(0, PLANE - 1)
    def _(n):
        send(piece(spot), piece(spot), b3_s, b3_r, in_plane(z, plane_peer(n), core)).start()

    @pl.loop(0, 2)
    def _(c):
        halo_x(c).wait_recv()
        halo_y(c).start()

    most = (PLANE - 1) * PIECE
    wait_bytes(kv.at[0, pl.ds(0, most)], b3_r)
    whole = kv.at[core, pl.ds(3 * ROWS, ROWS)]
    prompt = send(whole, whole, b4_s, b4_r, other_core)
    prompt.start()

    @pl.loop(2, PAIRS)
    def _(c):
        halo_x(c).wait_recv()
        halo_y(c).start()

    prompt.wait()

    def y_back(c):
        return send(ys.at[:, :, columns(c)], yr.at[:, :, columns(c)], y_s.at[c], y_r.at[c], behind)

    def x_back(c):
        return send(xs.at[:, :, columns(c)], xr.at[:, :, columns(c)], x_s.at[c], x_r.at[c], partner)

    def swap(c):
        return send(ps.at[1 - core, :, columns(c)], pr.at[:, columns(c)], r1_s.at[c], r1_r.at[c], other_core)

    def scatter(c, n):
        to = plane_peer(n)
        return send(
            rb.at[pl.ds(pl.multiple_of(to * PIECE, PIECE), PIECE), columns(c)],
            rc.at[spot, :, columns(c)], r2_s.at[c], r2_r.at[c], in_plane(z, to, core),
        )

    def sink(c):
        return send(pz.at[:, columns(c)], rz.at[z, :, columns(c)], r3_s.at[c], r3_r.at[c], in_column(0))

    def place():
        return pl.ds(pl.multiple_of(core * ROWS + spot * PIECE, PIECE), PIECE)

    def collect(c):
        return send(pf.at[:, columns(c)], rf.at[place(), columns(c)], r4_s.at[c], r4_r.at[c], root)

    @pl.loop(0, PAIRS + 4)
    def _(t):
        @pl.when(t < PAIRS)
        def _():
            halo_y(t).wait_recv()
            attend_pair(t, q, g, kv, bias, kt, vt, gt, x, e, dk, dv, att_t, dq_t, att, dq)
            cols = columns(t)
            for n, grad, scale in ((0, dk, SCALE), (1, dv, 1.0)):
                ys[n, :, cols] = (grad[pl.ds(far, ROWS), :] * scale).astype(BF)
                xs[n, :, cols] = (grad[pl.ds(near, ROWS), :] * scale).astype(BF)
                own[n, :, cols] = grad[pl.ds(ROWS, ROWS), :] * scale
                ps[n, :, cols] = (grad[pl.ds(3 * ROWS, ROWS), :] * scale).astype(BF)
            y_back(t).start()
            swap(t).start()

        @pl.when(jnp.logical_and(t >= 1, t < PAIRS + 1))
        def _():
            c = t - 1
            cols = columns(c)
            swap(c).wait_recv()
            rb[:, cols] = (ps[core, :, cols].astype(F32) + pr[:, cols].astype(F32)).astype(BF)

            @pl.loop(0, PLANE - 1)
            def _(n):
                scatter(c, n).start()

            y_back(c).wait_recv()
            for n in range(2):
                xs[n, :, cols] = (xs[n, :, cols].astype(F32) + yr[n, :, cols].astype(F32)).astype(BF)
            x_back(c).start()

        @pl.when(jnp.logical_and(t >= 2, t < PAIRS + 2))
        def _():
            c = t - 2
            cols = columns(c)
            wait_bytes(rc.at[pl.ds(0, PLANE - 1), :, columns(0)], r2_r.at[c])
            rc[spot, :, cols] = rb[pl.ds(pl.multiple_of(spot * PIECE, PIECE), PIECE), cols]
            part = rc[0, :, cols].astype(F32)
            for n in range(1, PLANE):
                part = part + rc[n, :, cols].astype(F32)
            pz[:, cols] = part

            @pl.when(jnp.logical_not(bottom))
            def _():
                sink(c).start()

            x_back(c).wait_recv()
            for n in range(2):
                own[n, :, cols] += xr[n, :, cols].astype(F32)

        @pl.when(jnp.logical_and(bottom, jnp.logical_and(t >= 3, t < PAIRS + 3)))
        def _():
            c = t - 3
            cols = columns(c)
            wait_bytes(rz.at[pl.ds(1, 7), :, columns(0)], r3_r.at[c])
            part = pz[:, cols]
            for n in range(1, 8):
                part = part + rz[n, :, cols]
            pf[:, cols] = part

            @pl.when(first)
            def _():
                rf[pl.ds(0, PIECE), cols] = part

            @pl.when(jnp.logical_not(first))
            def _():
                collect(c).start()

        @pl.when(jnp.logical_and(first, t >= 4))
        def _():
            c = t - 4
            cols = columns(c)
            wait_bytes(rf.at[pl.ds(0, (2 * PLANE - 1) * PIECE), columns(0)], r4_r.at[c])
            for n in range(2):
                own[n, :, cols] += rf[pl.ds(n * ROWS, ROWS), cols]

    out_k[...] = own[0].astype(BF)
    out_v[...] = own[1].astype(BF)

    @pl.loop(0, PAIRS)
    def _(c):
        halo_x(c).wait_send()
        halo_y(c).wait_send()
        y_back(c).wait_send()
        x_back(c).wait_send()
        swap(c).wait_send()
        wait_bytes(rc.at[pl.ds(0, PLANE - 1), :, columns(0)], r2_s.at[c])

        @pl.when(jnp.logical_not(bottom))
        def _():
            sink(c).wait_send()

        @pl.when(jnp.logical_and(bottom, jnp.logical_not(first)))
        def _():
            collect(c).wait_send()

    wait_bytes(kv.at[0, pl.ds(0, most)], b3_s)

    @pl.when(bottom)
    def _():
        wait_bytes(kv.at[0, pl.ds(0, 7 * PIECE)], b2_s)

    @pl.when(first)
    def _():
        wait_bytes(kv.at[0, pl.ds(0, (2 * PLANE - 1) * PIECE)], b1_s)


def on_device(query, keys, values, grad_out, band, prefix_len):
    vmem = pl.BlockSpec(memory_space=pltpu.VMEM)
    smem = pl.BlockSpec(memory_space=pltpu.SMEM)
    hbm = pl.BlockSpec(memory_space=pl.ANY)
    dma = pltpu.SemaphoreType.DMA
    return pl.pallas_call(
        kernel,
        out_shape=[jax.ShapeDtypeStruct((ROWS, WIDTH), BF)] * 4,
        in_specs=[smem, smem, vmem, hbm, hbm, vmem],
        out_specs=[vmem] * 4,
        scratch_shapes=[
            pltpu.VMEM((2, CAND, WIDTH), BF),
            pltpu.VMEM((2, KEYS, PAIR), F32),
            pltpu.VMEM((PAIR, CAND), BF),
            pltpu.VMEM((PAIR, CAND), BF),
            pltpu.VMEM((PAIR, ROWS), BF),
            pltpu.VMEM((KEYS, BLK), F32),
            pltpu.VMEM((KEYS, BLK), BF),
            pltpu.VMEM((CAND, PAIR), F32),
            pltpu.VMEM((CAND, PAIR), F32),
            pltpu.VMEM((PAIR, BLK), F32),
            pltpu.VMEM((PAIR, BLK), F32),
            pltpu.VMEM((2, ROWS, WIDTH), F32),
            pltpu.VMEM((2, ROWS, WIDTH), BF),
            pltpu.VMEM((2, ROWS, WIDTH), BF),
            pltpu.VMEM((2, ROWS, WIDTH), BF),
            pltpu.VMEM((2, ROWS, WIDTH), BF),
            pltpu.VMEM((2, ROWS, WIDTH), BF),
            pltpu.VMEM((ROWS, WIDTH), BF),
            pltpu.VMEM((ROWS, WIDTH), BF),
            pltpu.VMEM((PLANE, PIECE, WIDTH), BF),
            pltpu.VMEM((PIECE, WIDTH), F32),
            pltpu.VMEM((8, PIECE, WIDTH), F32),
            pltpu.VMEM((PIECE, WIDTH), F32),
            pltpu.VMEM((2 * ROWS, WIDTH), F32),
            dma((2,)),
            dma((PAIRS,)), dma((PAIRS,)), dma((PAIRS,)), dma((PAIRS,)),
            dma, dma, dma, dma, dma, dma, dma, dma,
            dma((PAIRS,)), dma((PAIRS,)), dma((PAIRS,)), dma((PAIRS,)),
            dma((PAIRS,)), dma((PAIRS,)), dma((PAIRS,)), dma((PAIRS,)),
            dma((PAIRS,)), dma((PAIRS,)), dma((PAIRS,)), dma((PAIRS,)),
        ],
        compiler_params=pltpu.CompilerParams(
            collective_id=0, has_side_effects=True, vmem_limit_bytes=58 * 2**20
        ),
        name="banded",
    )(band, prefix_len, query, keys, values, grad_out)


def solution(mesh):
    rows = P(("outer", "inner"), None)
    return jax.shard_map(
        on_device,
        mesh=mesh,
        in_specs=(rows, rows, rows, rows, rows, P()),
        out_specs=(rows, rows, rows, rows),
        check_vma=False,
    )
```

time: 710 us -> 129 us (0.18)
  waiting for transfers between devices: 556 us -> 0 us
  Pallas kernels: 0 us -> 122 us
  matrix products: 75.7 us -> 0 us
  other arithmetic: 22 us -> 0 us
  local copies, waits for them, and re-layouts: 26.8 us -> 5.18 us
  between operations: 14.9 us -> 1.3 us
  starting transfers between devices: 11.8 us -> 0 us
    psum x2 -> x0, waiting for transfers between devices: 556 us -> none  [the longest x1 285 us: on_device(): summed = lax.psum(prompt_parts, ('outer', 'inner'))]
    pallas_call x0 -> x1, Pallas kernels: none -> 122 us  [on_device(): pl.pallas_call(kernel, out_shape=[jax.ShapeDtypeStruct((ROWS, WIDTH), BF)...]
    dot_general x20 -> x0, matrix products: 50.9 us -> none  [the longest x4 18.5 us: attend_pair(): jnp.einsum('qhd,khd->hqk', grad_out, cand_v, preferred_element_type=jnp.f...]
    sub x4 -> x0, matrix products: 24.8 us -> none  [attend_pair(): expo = jnp.exp(scores - top)]
    another operation x8 -> x0, other arithmetic: 13 us -> none
    while x33 -> x0, local copies, waits for them, and re-layouts: 11.9 us -> none
    ppermute x4 -> x0, starting transfers between devices: 11.8 us -> none  [shifted(): return lax.ppermute(shard, axis, pairs)]
  transfers between devices with their start and end apart: 6 -> 0, of which waited for: 2 -> 0; matrix products, arithmetic and copies ran while one was open for 1% -> 0% of each run, Pallas kernels for 0% -> 0%
where the time goes in v1:
time: 129 us
  Pallas kernels  122 us (95%)
  local copies, waits for them, and re-layouts  5.18 us (4%)
  between operations  1.3 us (1%)
    pallas_call x1, Pallas kernels, on_device(): pl.pallas_call(kernel, out_shape=[jax.ShapeDtypeStruct((ROWS, WIDTH), BF)...  122 us
    unnamed x10, local copies, waits for them, and re-layouts  5.18 us

profile of v1, /device:TPU:0, one launch (start us, length us, event | category | flops | bytes accessed | tf_op | source)
XLA Modules:
  0.0 128.8 jit_solution(8920388735984125319)
XLA Ops:
  1.3 122.3 %banded.1 = (bf16[512,512]{1,0:T(8,128)(2,1)}, bf16[512,512]{1,0:T(8,128)(2,1)}, bf16[512,512]{1,0:T(8,128)(2,1)}, bf16[512,512]{1,0:T(8,128)(2,1)}) custom-call(s32[2,5]{1,0:T(2,128)} %band.1, s32[1]{0:T(128)S(6)} %copy.14.plen, bf16[512,512]{1,0:T(8,128)(2,1)} %q.1, bf16[512,512]{1,0:T(8,128)(2,1)} %k.1, bf16[512,512]{1,0:T(8,128)(2,1)} %v.1, ...), custom_call_target="tpu_custom_call" | custom-call | tf_op jit(solution)/shard_map/banded/pallas_call | solution.py:416
  123.6 0.0 copy-start.2
  123.6 1.9 %copy.15 = bf16[512,512]{1,0:T(8,128)(2,1)} copy(bf16[512,512]{1,0:T(8,128)(2,1)} %get-tuple-element.8) | data formatting | bytes 1048576
  125.6 0.0 copy-done.2
  125.6 0.0 copy-start.1
  125.6 0.8 copy.16
  126.4 0.4 copy-done.1
  126.8 0.0 copy-start
  126.8 0.8 copy.17
  127.6 0.4 copy-done
  128.0 0.8 copy.18
Async XLA Ops:
  123.6 1.9 %copy-start.2 = (bf16[512,512]{1,0:T(8,128)(2,1)S(1)}, bf16[512,512]{1,0:T(8,128)(2,1)}, u32[]{:S(2)}) copy-start(bf16[512,512]{1,0:T(8,128)(2,1)} %get-tuple-element.9) | copy-start | bytes 1572868
  125.6 1.2 copy-start.1
  126.8 1.2 copy-start

commit v2 on v1

v2 whole, which is shorter than its diff:
```python
import functools

import jax
import jax.numpy as jnp
from jax import lax
from jax.experimental import pallas as pl
from jax.experimental.pallas import tpu as pltpu
from jax.sharding import PartitionSpec as P

F32 = jnp.float32
BF = jnp.bfloat16
MESH = pl.DeviceIdType.MESH
BLK = 256
ROWS = 512
WIDTH = 512
PAIR = 128
PAIRS = 2
HEAD = 64
SLOTS = 5
TILES = 7
KEYS = TILES * BLK
CAND = 2560
PROMPT = 2048
MINE = 256
SCALE = HEAD ** -0.5
TO_EXP2 = SCALE * 1.4426950408889634
OFF = -1e30
PLANE = 8
PIECE = 64


def dot_last(a, b):
    return lax.dot_general(a, b, (((1,), (1,)), ((), ())), preferred_element_type=F32)


def dot(a, b):
    return lax.dot_general(a, b, (((1,), (0,)), ((), ())), preferred_element_type=F32)


def at_block(start):
    return pl.ds(pl.multiple_of(start, BLK), BLK)


def fill_bias(listed, plen, bias, base):
    row = lax.broadcasted_iota(jnp.int32, (BLK, PAIR), 0)
    for i in range(4):
        for s in range(SLOTS):
            ok = (base + i - 2 + s) * BLK + row >= plen[0]
            n = (i % 2) * SLOTS + s
            bias[i, s * BLK : (s + 1) * BLK, :] = jnp.where(ok, listed[i // 2, n : n + 1, :], OFF)
        for s in range(2):
            low = (SLOTS + s) * BLK
            bias[i, low : low + BLK, :] = jnp.where(row + s * BLK < plen[0], 0.0, OFF)


def attend(p, u, kv, qg, bias, kt, vt, gt, x, e, dk, dv, att_t, dq_t, result):
    cols = pl.ds(pl.multiple_of(p * PAIR, PAIR), PAIR)
    lane = lax.broadcasted_iota(jnp.int32, (BLK, PAIR), 1)
    combos = [(qb, h) for qb in range(2) for h in range(2)]

    def half(h):
        return (lane < HEAD) if h == 0 else (lane >= HEAD)

    def heads(h):
        return slice(h * HEAD, (h + 1) * HEAD)

    def mine(qb):
        return at_block(u * ROWS + qb * BLK)

    def keys_of(qb, s):
        return at_block(u * ROWS + (qb + s) * BLK) if s < SLOTS else at_block(PROMPT + (s - SLOTS) * BLK)

    qz = [jnp.where(half(h), qg[0, mine(qb), cols], jnp.zeros((), BF)) for qb, h in combos]

    def score(n):
        qb, h = combos[n]
        top = jnp.full((8, BLK), OFF, F32)
        for s in range(TILES):
            t = dot_last(kv[0, keys_of(qb, s), cols], qz[n]) * TO_EXP2
            b = bias[2 * u + qb, s * BLK : (s + 1) * BLK, :]
            t = t + jnp.concatenate([b, b], axis=1)
            x[n, s * BLK : (s + 1) * BLK, :] = t
            top = jnp.maximum(top, jnp.max(t.reshape(BLK // 8, 8, BLK), axis=0))
        return jnp.max(top, axis=0, keepdims=True)

    def weigh(n, top):
        qb, h = combos[n]
        total = jnp.zeros((8, BLK), F32)
        a = jnp.zeros((HEAD, BLK), F32)
        for s in range(TILES):
            expo = jnp.exp2(x[n, s * BLK : (s + 1) * BLK, :] - top)
            total = total + jnp.sum(expo.reshape(BLK // 8, 8, BLK), axis=0)
            eb = expo.astype(BF)
            e[n, s * BLK : (s + 1) * BLK, :] = eb
            a = a + dot(vt[heads(h), keys_of(qb, s)], eb)
        r = 1.0 / jnp.sum(total, axis=0, keepdims=True)
        a = a * r
        att_t[qb, heads(h), :] = a
        r_col = jnp.broadcast_to(r, (PAIR, BLK)).T
        gz = jnp.where(half(h), qg[1, mine(qb), cols].astype(F32) * r_col, 0.0).astype(BF)
        g_row = (gt[heads(h), mine(qb)].astype(F32) * r).astype(BF).astype(F32)
        return gz, jnp.sum(g_row * a, axis=0, keepdims=True)

    def differentiate(n, gz, delta):
        qb, h = combos[n]
        d = jnp.zeros((HEAD, BLK), F32)
        band_rows = pl.ds(pl.multiple_of(u * ROWS + qb * BLK, BLK), SLOTS * BLK)
        for low, count, rows in ((0, SLOTS * BLK, band_rows), (SLOTS * BLK, 2 * BLK, pl.ds(PROMPT, 2 * BLK))):
            eb = e[n, low : low + count, :]
            dp = dot_last(kv[1, rows, cols], gz) - delta
            ds = (eb.astype(F32) * dp).astype(BF)
            dv[rows, :] += dot(eb, gz)
            dk[rows, :] += dot(ds, qz[n])
            d = d + dot(kt[heads(h), rows], ds)
        dq_t[qb, heads(h), :] = d * SCALE

    tops = [score(0)]
    grads = []
    for n in range(4):
        if n < 3:
            tops.append(score(n + 1))
        grads.append(weigh(n, tops[n]))
        if n >= 1:
            differentiate(n - 1, *grads[n - 1])
    differentiate(3, *grads[3])
    for qb in range(2):
        result[0, mine(qb), cols] = att_t[qb].T.astype(BF)
        result[1, mine(qb), cols] = dq_t[qb].T.astype(BF)


def wait_bytes(ref, sem):
    pltpu.make_async_copy(ref, ref, sem).wait()


def kernel(
    band, plen, q, k, v, g, att, dq, out_k, out_v,
    kv, qg, listed, bias, kt, vt, gt, x, e, dk, dv, att_t, dq_t, result,
    own, near_s, near_r, far_s, far_r, xo, xr, ps, pr, rb, ry, pz, rz, pf, rf,
    local_sem, l_s, l_r, x_s, x_r, e_s, e_r, f_s, f_r,
    b1_s, b1_r, b2_s, b2_r, b3_s, b3_r, b4_s, b4_r,
    n_s, n_r, w_s, w_r, o_s, o_r, r1_s, r1_r, r2_s, r2_r, r3_s, r3_r, r4_s, r4_r,
):
    outer = lax.axis_index("outer")
    inner = lax.axis_index("inner")
    device = outer * 8 + inner
    z = outer // 4
    x_lo = (outer // 2) % 2
    core = outer % 2
    side = inner % 2
    spot = (inner // 2) * 2 + x_lo
    partner = (outer, inner + 1 - 2 * side)
    up = lax.rem(device + 2, 256)
    down = lax.rem(device + 254, 256)
    near = jnp.where(side == 0, down, up)
    far = jnp.where(side == 0, up, down)
    near = (near // 8, near % 8)
    far = (far // 8, far % 8)
    other_core = (outer + 1 - 2 * core, inner)
    root = (0, 0)
    first = device == 0
    bottom = z == 0

    def in_plane(level, at, part, which):
        return ((level * 2 + at % 2) * 2 + which, (at // 2) * 2 + part)

    def in_column(level):
        return ((level * 2 + x_lo) * 2 + core, inner)

    def peer(n):
        return lax.rem(spot + n, PLANE)

    def lanes(part):
        return pl.ds(pl.multiple_of(part * MINE, MINE), MINE)

    def columns(c):
        return pl.ds(pl.multiple_of(c * PAIR, PAIR), PAIR)

    def run(part):
        return pl.ds(pl.multiple_of(part * ROWS, ROWS), ROWS)

    own_rows = run(1 + side)
    near_rows = pl.ds(pl.multiple_of((1 - side) * 3 * ROWS, ROWS), ROWS)
    far_rows = pl.ds(pl.multiple_of(side * 3 * ROWS, ROWS), ROWS)
    held = [(k, kv.at[0], own_rows), (v, kv.at[1], own_rows), (q, qg.at[0], run(side)), (g, qg.at[1], run(side))]
    mine_in = [
        pltpu.make_async_copy(src.at[:, lanes(side)], dst.at[rows], local_sem.at[n])
        for n, (src, dst, rows) in enumerate(held)
    ]
    for c in mine_in:
        c.start()
    for qb in range(2):
        for s in range(SLOTS):
            n = qb * SLOTS + s
            listed[side, n : n + 1, :] = jnp.full((1, PAIR), jnp.where(band[qb, s] >= 0, 0.0, OFF), F32)
    for n in range(2 * SLOTS, 16):
        listed[side, n : n + 1, :] = jnp.zeros((1, PAIR), F32)

    barrier = pltpu.get_barrier_semaphore()

    def hello(target):
        pl.semaphore_signal(barrier, inc=1, device_id=target, device_id_type=MESH)

    for target in (partner, near, far, other_core):
        hello(target)
    for n in range(1, PLANE):
        hello(in_plane(z, peer(n), side, core))

    @pl.when(bottom)
    def _():
        @pl.loop(1, 8)
        def _(n):
            hello(in_column(n))

    @pl.when(jnp.logical_not(bottom))
    def _():
        hello(in_column(0))

    def root_peer(n):
        return in_plane(0, n % PLANE, (n // PLANE) % 2, n // (2 * PLANE))

    @pl.when(first)
    def _():
        @pl.loop(1, 4 * PLANE)
        def _(n):
            hello(root_peer(n))

    @pl.when(jnp.logical_and(bottom, jnp.logical_not(first)))
    def _():
        hello(root)

    greeted = 4 + PLANE - 1 + jnp.where(bottom, 7, 1)
    greeted = greeted + jnp.where(first, 4 * PLANE - 1, jnp.where(bottom, 1, 0))
    for c in mine_in:
        c.wait()
    pl.semaphore_wait(barrier, greeted)

    def send(src, dst, s_sem, r_sem, target):
        return pltpu.make_async_remote_copy(
            src_ref=src, dst_ref=dst, send_sem=s_sem, recv_sem=r_sem,
            device_id=target, device_id_type=MESH,
        )

    def cross(c):
        lane = pl.ds(pl.multiple_of((1 - side) * MINE + c * PAIR, PAIR), PAIR)
        return [
            send(src.at[:, lane], dst.at[rows, columns(c)], x_s.at[4 * c + n], x_r.at[4 * c + n], partner)
            for n, (src, dst, rows) in enumerate(held)
        ]

    def to_near(c):
        return send(
            kv.at[:, own_rows, columns(c)], kv.at[:, near_rows, columns(c)], e_s.at[c], e_r.at[c], near
        )

    def to_far(c):
        return send(
            kv.at[:, run(2 - side), columns(c)], kv.at[:, far_rows, columns(c)], f_s.at[c], f_r.at[c], far
        )

    def strip(at):
        return pl.ds(pl.multiple_of(at * PIECE, PIECE), PIECE)

    def piece(which, at):
        return kv.at[which, pl.ds(pl.multiple_of(PROMPT + at * PIECE, PIECE), PIECE)]

    @pl.when(first)
    def _():
        for which, src, low in ((0, k, 1), (1, v, 0)):

            @pl.loop(low, 2 * PLANE)
            def _(n):
                at = n % PLANE
                send(
                    src.at[strip(at), lanes(n // PLANE)], piece(which, at), b1_s, b1_r,
                    root_peer(n + which * 2 * PLANE),
                ).start()

        own_piece = pltpu.make_async_copy(k.at[strip(0), lanes(0)], piece(0, 0), local_sem.at[0])
        own_piece.start()
        own_piece.wait()

    note = send(listed.at[side], listed.at[side], l_s, l_r, partner)
    note.start()
    for c in cross(0):
        c.start()
    to_near(0).start()

    @pl.when(jnp.logical_and(bottom, jnp.logical_not(first)))
    def _():
        wait_bytes(piece(core, spot), b1_r)

    @pl.when(bottom)
    def _():
        @pl.loop(1, 8)
        def _(n):
            send(piece(core, spot), piece(core, spot), b2_s, b2_r, in_column(n)).start()

    note.wait()
    fill_bias(listed, plen, bias, 2 * (device - side))

    @pl.when(jnp.logical_not(bottom))
    def _():
        wait_bytes(piece(core, spot), b2_r)

    for n in range(1, PLANE):
        send(piece(core, spot), piece(core, spot), b3_s, b3_r, in_plane(z, peer(n), side, core)).start()
    for c in cross(0):
        c.wait_recv()
    to_far(0).start()
    for c in cross(1):
        c.start()
    to_near(1).start()
    wait_bytes(kv.at[0, pl.ds(0, (PLANE - 1) * PIECE)], b3_r)
    whole = kv.at[core, pl.ds(PROMPT, ROWS)]
    prompt = send(whole, whole, b4_s, b4_r, other_core)
    prompt.start()
    prompt.wait()

    def near_back(c):
        return send(near_s.at[:, :, columns(c)], near_r.at[:, :, columns(c)], n_s.at[c], n_r.at[c], near)

    def far_back(c):
        return send(far_s.at[:, :, columns(c)], far_r.at[:, :, columns(c)], w_s.at[c], w_r.at[c], far)

    def x_back(c):
        return [
            send(result.at[:, run(1 - side), columns(c)], xr.at[0:2, :, columns(c)], o_s.at[2 * c], o_r.at[2 * c], partner),
            send(xo.at[:, :, columns(c)], xr.at[2:4, :, columns(c)], o_s.at[2 * c + 1], o_r.at[2 * c + 1], partner),
        ]

    def swap(c):
        return send(ps.at[1 - core, :, columns(c)], pr.at[:, columns(c)], r1_s.at[c], r1_r.at[c], other_core)

    def scatter(c, n):
        to = peer(n)
        return send(
            rb.at[strip(to), columns(c)], ry.at[spot, :, columns(c)], r2_s.at[c], r2_r.at[c],
            in_plane(z, to, side, core),
        )

    def sink(c):
        return send(pz.at[:, columns(c)], rz.at[z, :, columns(c)], r3_s.at[c], r3_r.at[c], in_column(0))

    def collect(c):
        place = pl.ds(pl.multiple_of(core * ROWS + spot * PIECE, PIECE), PIECE)
        lane = pl.ds(pl.multiple_of(side * MINE + c * PAIR, PAIR), PAIR)
        return send(pf.at[:, columns(c)], rf.at[place, lane], r4_s.at[c], r4_r.at[c], root)

    def hand_back(c):
        cols = columns(c)
        x_back(c)[0].start()
        for n, grad, scale in ((0, dk, SCALE), (1, dv, 1.0)):
            ps[n, :, cols] = (grad[pl.ds(PROMPT, ROWS), :] * scale).astype(BF)
        swap(c).start()
        for n, grad, scale in ((0, dk, SCALE), (1, dv, 1.0)):
            far_s[n, :, cols] = (grad[near_back_rows[1], :] * scale).astype(BF)
        far_back(c).start()
        near_back(c).wait_recv()
        for n, grad, scale in ((0, dk, SCALE), (1, dv, 1.0)):
            xo[n, :, cols] = (grad[run(2 - side), :] * scale + near_r[n, :, cols].astype(F32)).astype(BF)
        x_back(c)[1].start()
        for n, grad, scale in ((0, dk, SCALE), (1, dv, 1.0)):
            own[n, :, cols] = grad[own_rows, :] * scale

    near_back_rows = (far_rows, near_rows)

    def reduce_plane(c):
        cols = columns(c)
        swap(c).wait_recv()
        rb[:, cols] = (ps[core, :, cols].astype(F32) + pr[:, cols].astype(F32)).astype(BF)
        for n in range(1, PLANE):
            scatter(c, n).start()

    def reduce_column(c):
        cols = columns(c)
        wait_bytes(ry.at[pl.ds(0, PLANE - 1), :, columns(0)], r2_r.at[c])
        ry[spot, :, cols] = rb[strip(spot), cols]
        part = ry[0, :, cols].astype(F32)
        for n in range(1, PLANE):
            part = part + ry[n, :, cols].astype(F32)
        pz[:, cols] = part

        @pl.when(jnp.logical_not(bottom))
        def _():
            sink(c).start()

    def reduce_root(c):
        cols = columns(c)

        @pl.when(bottom)
        def _():
            wait_bytes(rz.at[pl.ds(1, 7), :, columns(0)], r3_r.at[c])
            part = pz[:, cols]
            for n in range(1, 8):
                part = part + rz[n, :, cols]
            pf[:, cols] = part

            @pl.when(first)
            def _():
                rf[pl.ds(0, PIECE), cols] = part

            @pl.when(jnp.logical_not(first))
            def _():
                collect(c).start()

    def settle(c):
        cols = columns(c)
        far_back(c).wait_recv()
        for n in range(2):
            own[n, :, cols] += far_r[n, :, cols].astype(F32)

    @pl.loop(0, 4)
    def _(t):
        p = t // 2
        late = t % 2

        @pl.when(late == 0)
        def _():
            to_near(p).wait_recv()
            dk[...] = jnp.zeros_like(dk)
            dv[...] = jnp.zeros_like(dv)

            to_far(p).wait_recv()
            cols = columns(p)
            kt[...] = kv[0, :, cols].T
            vt[...] = kv[1, :, cols].T
            gt[...] = qg[1, :, cols].T

        @pl.when(t == 1)
        def _():
            for c in cross(1):
                c.wait_recv()
            to_far(1).start()

        u = jnp.where(late == 0, side, 1 - side)
        attend(p, u, kv, qg, bias, kt, vt, gt, x, e, dk, dv, att_t, dq_t, result)

        @pl.when(late == 0)
        def _():
            cols = columns(p)
            for n, grad, scale in ((0, dk, SCALE), (1, dv, 1.0)):
                near_s[n, :, cols] = (grad[near_back_rows[0], :] * scale).astype(BF)
            near_back(p).start()

        @pl.when(t == 1)
        def _():
            hand_back(0)

        @pl.when(t == 2)
        def _():
            reduce_plane(0)

        @pl.when(t == 3)
        def _():
            hand_back(1)
            reduce_column(0)

    reduce_plane(1)
    reduce_root(0)
    settle(0)
    reduce_column(1)
    for n, ref in ((0, att), (1, dq)):
        ref[:, lanes(side)] = result[n, run(side), :]
    settle(1)
    reduce_root(1)
    for c in range(PAIRS):
        for copy in x_back(c):
            copy.wait_recv()

    @pl.when(first)
    def _():
        for c in range(PAIRS):
            wait_bytes(rf.at[pl.ds(0, (4 * PLANE - 1) * PIECE // 2), lanes(0)], r4_r.at[c])
        for n in range(2):
            own[n] += rf[pl.ds(n * ROWS, ROWS), lanes(0)]
            xr[2 + n] = (xr[2 + n].astype(F32) + rf[pl.ds(n * ROWS, ROWS), lanes(1)]).astype(BF)

    for n, ref in enumerate((att, dq, out_k, out_v)):
        ref[:, lanes(1 - side)] = xr[n]
    for n, ref in ((0, out_k), (1, out_v)):
        ref[:, lanes(side)] = own[n].astype(BF)

    for c in range(PAIRS):
        for copy in cross(c) + x_back(c):
            copy.wait_send()
        for copy in (to_near(c), to_far(c), near_back(c), far_back(c), swap(c)):
            copy.wait_send()
        wait_bytes(ry.at[pl.ds(0, PLANE - 1), :, columns(0)], r2_s.at[c])

        @pl.when(jnp.logical_not(bottom))
        def _(c=c):
            sink(c).wait_send()

        @pl.when(jnp.logical_and(bottom, jnp.logical_not(first)))
        def _(c=c):
            collect(c).wait_send()

    wait_bytes(kv.at[0, pl.ds(0, (PLANE - 1) * PIECE)], b3_s)

    @pl.when(bottom)
    def _():
        wait_bytes(kv.at[0, pl.ds(0, 7 * PIECE)], b2_s)

    @pl.when(first)
    def _():
        wait_bytes(kv.at[0, pl.ds(0, (4 * PLANE - 1) * PIECE)], b1_s)


def on_device(query, keys, values, grad_out, band, prefix_len):
    vmem = pl.BlockSpec(memory_space=pltpu.VMEM)
    smem = pl.BlockSpec(memory_space=pltpu.SMEM)
    hbm = pl.BlockSpec(memory_space=pl.ANY)
    dma = pltpu.SemaphoreType.DMA
    two = dma((PAIRS,))
    return pl.pallas_call(
        kernel,
        out_shape=[jax.ShapeDtypeStruct((ROWS, WIDTH), BF)] * 4,
        in_specs=[smem, smem, hbm, hbm, hbm, hbm],
        out_specs=[vmem] * 4,
        scratch_shapes=[
            pltpu.VMEM((2, CAND, MINE), BF),
            pltpu.VMEM((2, 2 * ROWS, MINE), BF),
            pltpu.VMEM((2, 16, PAIR), F32),
            pltpu.VMEM((4, KEYS, PAIR), F32),
            pltpu.VMEM((PAIR, CAND), BF),
            pltpu.VMEM((PAIR, CAND), BF),
            pltpu.VMEM((PAIR, 2 * ROWS), BF),
            pltpu.VMEM((4, KEYS, BLK), F32),
            pltpu.VMEM((4, KEYS, BLK), BF),
            pltpu.VMEM((CAND, PAIR), F32),
            pltpu.VMEM((CAND, PAIR), F32),
            pltpu.VMEM((2, PAIR, BLK), F32),
            pltpu.VMEM((2, PAIR, BLK), F32),
            pltpu.VMEM((2, 2 * ROWS, MINE), BF),
            pltpu.VMEM((2, ROWS, MINE), F32),
            pltpu.VMEM((2, ROWS, MINE), BF),
            pltpu.VMEM((2, ROWS, MINE), BF),
            pltpu.VMEM((2, ROWS, MINE), BF),
            pltpu.VMEM((2, ROWS, MINE), BF),
            pltpu.VMEM((2, ROWS, MINE), BF),
            pltpu.VMEM((4, ROWS, MINE), BF),
            pltpu.VMEM((2, ROWS, MINE), BF),
            pltpu.VMEM((ROWS, MINE), BF),
            pltpu.VMEM((ROWS, MINE), BF),
            pltpu.VMEM((PLANE, PIECE, MINE), BF),
            pltpu.VMEM((PIECE, MINE), F32),
            pltpu.VMEM((8, PIECE, MINE), F32),
            pltpu.VMEM((PIECE, MINE), F32),
            pltpu.VMEM((2 * ROWS, WIDTH), F32),
            dma((4,)), dma, dma, dma((4 * PAIRS,)), dma((4 * PAIRS,)), two, two, two, two,
            dma, dma, dma, dma, dma, dma, dma, dma,
            two, two, two, two, dma((2 * PAIRS,)), dma((2 * PAIRS,)),
            two, two, two, two, two, two, two, two,
        ],
        compiler_params=pltpu.CompilerParams(
            collective_id=0, has_side_effects=True, vmem_limit_bytes=58 * 2**20
        ),
        name="banded",
    )(band, prefix_len, query, keys, values, grad_out)


def solution(mesh):
    rows = P(("outer", "inner"), None)
    return jax.shard_map(
        on_device,
        mesh=mesh,
        in_specs=(rows, rows, rows, rows, rows, P()),
        out_specs=(rows, rows, rows, rows),
        check_vma=False,
    )
```

time: 129 us -> 110 us (0.85)
  Pallas kernels: 122 us -> 103 us
    pallas_call x1, Pallas kernels: 122 us -> 103 us  [on_device(): pl.pallas_call(kernel, out_shape=[jax.ShapeDtypeStruct((ROWS, WIDTH), BF)...]
where the time goes in v2:
time: 110 us
  Pallas kernels  103 us (94%)
  local copies, waits for them, and re-layouts  5.18 us (5%)
  between operations  1.3 us (1%)
    pallas_call x1, Pallas kernels, on_device(): pl.pallas_call(kernel, out_shape=[jax.ShapeDtypeStruct((ROWS, WIDTH), BF)...  103 us
    unnamed x10, local copies, waits for them, and re-layouts  5.18 us

profile of v2, /device:TPU:0, one launch (start us, length us, event | category | flops | bytes accessed | tf_op | source)
XLA Modules:
  0.0 109.6 jit_solution(9513801677227179359)
XLA Ops:
  1.3 103.2 %banded.1 = (bf16[512,512]{1,0:T(8,128)(2,1)}, bf16[512,512]{1,0:T(8,128)(2,1)}, bf16[512,512]{1,0:T(8,128)(2,1)}, bf16[512,512]{1,0:T(8,128)(2,1)}) custom-call(s32[2,5]{1,0:T(2,128)} %band.1, s32[1]{0:T(128)S(6)} %copy.14.plen, bf16[512,512]{1,0:T(8,128)(2,1)} %q.1, bf16[512,512]{1,0:T(8,128)(2,1)} %k.1, bf16[512,512]{1,0:T(8,128)(2,1)} %v.1, ...), custom_call_target="tpu_custom_call" | custom-call | tf_op jit(solution)/shard_map/banded/pallas_call | solution.py:515
  104.4 0.0 copy-start.2
  104.5 1.9 %copy.15 = bf16[512,512]{1,0:T(8,128)(2,1)} copy(bf16[512,512]{1,0:T(8,128)(2,1)} %get-tuple-element.8) | data formatting | bytes 1048576
  106.4 0.0 copy-done.2
  106.4 0.0 copy-start.1
  106.4 0.8 copy.16
  107.2 0.4 copy-done.1
  107.6 0.0 copy-start
  107.6 0.8 copy.17
  108.4 0.4 copy-done
  108.8 0.8 copy.18
Async XLA Ops:
  104.4 1.9 %copy-start.2 = (bf16[512,512]{1,0:T(8,128)(2,1)S(1)}, bf16[512,512]{1,0:T(8,128)(2,1)}, u32[]{:S(2)}) copy-start(bf16[512,512]{1,0:T(8,128)(2,1)} %get-tuple-element.9) | copy-start | bytes 1572868
  106.4 1.2 %copy-start.1 = (bf16[512,512]{1,0:T(8,128)(2,1)S(1)}, bf16[512,512]{1,0:T(8,128)(2,1)}, u32[]{:S(2)}) copy-start(bf16[512,512]{1,0:T(8,128)(2,1)} %get-tuple-element.10) | copy-start | bytes 1572868
  107.6 1.2 %copy-start = (bf16[512,512]{1,0:T(8,128)(2,1)S(1)}, bf16[512,512]{1,0:T(8,128)(2,1)}, u32[]{:S(2)}) copy-start(bf16[512,512]{1,0:T(8,128)(2,1)} %get-tuple-element.11) | copy-start | bytes 1572868

commit v3 on v2

--- a/solution.py
+++ b/solution.py
@@ -53,7 +53,7 @@
             bias[i, low : low + BLK, :] = jnp.where(row + s * BLK < plen[0], 0.0, OFF)
 
 
-def attend(p, u, kv, qg, bias, kt, vt, gt, x, e, dk, dv, att_t, dq_t, result):
+def attend(p, u, kv, qg, bias, kt, vt, gt, x, e, dk, dv, att_t, dq_t, result, midway):
     cols = pl.ds(pl.multiple_of(p * PAIR, PAIR), PAIR)
     lane = lax.broadcasted_iota(jnp.int32, (BLK, PAIR), 1)
     combos = [(qb, h) for qb in range(2) for h in range(2)]
@@ -101,18 +101,23 @@
         g_row = (gt[heads(h), mine(qb)].astype(F32) * r).astype(BF).astype(F32)
         return gz, jnp.sum(g_row * a, axis=0, keepdims=True)
 
-    def differentiate(n, gz, delta):
+    def differentiate(n, gz, delta, low, count, rows):
         qb, h = combos[n]
-        d = jnp.zeros((HEAD, BLK), F32)
-        band_rows = pl.ds(pl.multiple_of(u * ROWS + qb * BLK, BLK), SLOTS * BLK)
-        for low, count, rows in ((0, SLOTS * BLK, band_rows), (SLOTS * BLK, 2 * BLK, pl.ds(PROMPT, 2 * BLK))):
-            eb = e[n, low : low + count, :]
-            dp = dot_last(kv[1, rows, cols], gz) - delta
-            ds = (eb.astype(F32) * dp).astype(BF)
-            dv[rows, :] += dot(eb, gz)
-            dk[rows, :] += dot(ds, qz[n])
-            d = d + dot(kt[heads(h), rows], ds)
-        dq_t[qb, heads(h), :] = d * SCALE
+        eb = e[n, low : low + count, :]
+        dp = dot_last(kv[1, rows, cols], gz) - delta
+        ds = (eb.astype(F32) * dp).astype(BF)
+        dv[rows, :] += dot(eb, gz)
+        dk[rows, :] += dot(ds, qz[n])
+        return dot(kt[heads(h), rows], ds) * SCALE
+
+    def on_prompt(n):
+        qb, h = combos[n]
+        dq_t[qb, heads(h), :] = differentiate(n, *grads[n], SLOTS * BLK, 2 * BLK, pl.ds(PROMPT, 2 * BLK))
+
+    def on_band(n):
+        qb, h = combos[n]
+        rows = pl.ds(pl.multiple_of(u * ROWS + qb * BLK, BLK), SLOTS * BLK)
+        dq_t[qb, heads(h), :] += differentiate(n, *grads[n], 0, SLOTS * BLK, rows)
 
     tops = [score(0)]
     grads = []
@@ -121,10 +126,14 @@
             tops.append(score(n + 1))
         grads.append(weigh(n, tops[n]))
         if n >= 1:
-            differentiate(n - 1, *grads[n - 1])
-    differentiate(3, *grads[3])
+            on_prompt(n - 1)
+    on_prompt(3)
     for qb in range(2):
         result[0, mine(qb), cols] = att_t[qb].T.astype(BF)
+    midway()
+    for n in range(4):
+        on_band(n)
+    for qb in range(2):
         result[1, mine(qb), cols] = dq_t[qb].T.astype(BF)
 
 
@@ -133,7 +142,7 @@
 
 
 def kernel(
-    band, plen, q, k, v, g, att, dq, out_k, out_v,
+    band, plen, q, k, v, g, out,
     kv, qg, listed, bias, kt, vt, gt, x, e, dk, dv, att_t, dq_t, result,
     own, near_s, near_r, far_s, far_r, xo, xr, ps, pr, rb, ry, pz, rz, pf, rf,
     local_sem, l_s, l_r, x_s, x_r, e_s, e_r, f_s, f_r,
@@ -304,11 +313,12 @@
 
     for n in range(1, PLANE):
         send(piece(core, spot), piece(core, spot), b3_s, b3_r, in_plane(z, peer(n), side, core)).start()
+    for c, later in zip(cross(0), cross(1)):
+        c.wait_send()
+        later.start()
     for c in cross(0):
         c.wait_recv()
     to_far(0).start()
-    for c in cross(1):
-        c.start()
     to_near(1).start()
     wait_bytes(kv.at[0, pl.ds(0, (PLANE - 1) * PIECE)], b3_r)
     whole = kv.at[core, pl.ds(PROMPT, ROWS)]
@@ -322,11 +332,12 @@
     def far_back(c):
         return send(far_s.at[:, :, columns(c)], far_r.at[:, :, columns(c)], w_s.at[c], w_r.at[c], far)
 
-    def x_back(c):
-        return [
-            send(result.at[:, run(1 - side), columns(c)], xr.at[0:2, :, columns(c)], o_s.at[2 * c], o_r.at[2 * c], partner),
-            send(xo.at[:, :, columns(c)], xr.at[2:4, :, columns(c)], o_s.at[2 * c + 1], o_r.at[2 * c + 1], partner),
-        ]
+    def x_back(c, n):
+        if n < 2:
+            src, dst = result.at[n, run(1 - side), columns(c)], xr.at[n, :, columns(c)]
+        else:
+            src, dst = xo.at[:, :, columns(c)], xr.at[2:4, :, columns(c)]
+        return send(src, dst, o_s.at[3 * c + n], o_r.at[3 * c + n], partner)
 
     def swap(c):
         return send(ps.at[1 - core, :, columns(c)], pr.at[:, columns(c)], r1_s.at[c], r1_r.at[c], other_core)
@@ -346,19 +357,24 @@
         lane = pl.ds(pl.multiple_of(side * MINE + c * PAIR, PAIR), PAIR)
         return send(pf.at[:, columns(c)], rf.at[place, lane], r4_s.at[c], r4_r.at[c], root)
 
-    def hand_back(c):
+    def hand_prompt(c):
         cols = columns(c)
-        x_back(c)[0].start()
         for n, grad, scale in ((0, dk, SCALE), (1, dv, 1.0)):
             ps[n, :, cols] = (grad[pl.ds(PROMPT, ROWS), :] * scale).astype(BF)
         swap(c).start()
+        x_back(c, 0).start()
+
+    def hand_back(c):
+        cols = columns(c)
+        reduce_plane(c)
         for n, grad, scale in ((0, dk, SCALE), (1, dv, 1.0)):
             far_s[n, :, cols] = (grad[near_back_rows[1], :] * scale).astype(BF)
         far_back(c).start()
+        x_back(c, 1).start()
         near_back(c).wait_recv()
         for n, grad, scale in ((0, dk, SCALE), (1, dv, 1.0)):
             xo[n, :, cols] = (grad[run(2 - side), :] * scale + near_r[n, :, cols].astype(F32)).astype(BF)
-        x_back(c)[1].start()
+        x_back(c, 2).start()
         for n, grad, scale in ((0, dk, SCALE), (1, dv, 1.0)):
             own[n, :, cols] = grad[own_rows, :] * scale
 
@@ -426,14 +442,22 @@
             vt[...] = kv[1, :, cols].T
             gt[...] = qg[1, :, cols].T
 
-        @pl.when(t == 1)
-        def _():
-            for c in cross(1):
-                c.wait_recv()
-            to_far(1).start()
-
         u = jnp.where(late == 0, side, 1 - side)
-        attend(p, u, kv, qg, bias, kt, vt, gt, x, e, dk, dv, att_t, dq_t, result)
+
+        def midway():
+            @pl.when(t == 0)
+            def _():
+                for c in cross(1):
+                    c.wait_recv()
+                to_far(1).start()
+
+            for c in range(PAIRS):
+
+                @pl.when(t == 2 * c + 1)
+                def _(c=c):
+                    hand_prompt(c)
+
+        attend(p, u, kv, qg, bias, kt, vt, gt, x, e, dk, dv, att_t, dq_t, result, midway)
 
         @pl.when(late == 0)
         def _():
@@ -448,24 +472,22 @@
 
         @pl.when(t == 2)
         def _():
-            reduce_plane(0)
+            reduce_column(0)
 
         @pl.when(t == 3)
         def _():
             hand_back(1)
-            reduce_column(0)
-
-    reduce_plane(1)
+
     reduce_root(0)
     settle(0)
     reduce_column(1)
-    for n, ref in ((0, att), (1, dq)):
-        ref[:, lanes(side)] = result[n, run(side), :]
+    for n in range(2):
+        out[n, :, lanes(side)] = result[n, run(side), :]
     settle(1)
     reduce_root(1)
     for c in range(PAIRS):
-        for copy in x_back(c):
-            copy.wait_recv()
+        for n in range(3):
+            x_back(c, n).wait_recv()
 
     @pl.when(first)
     def _():
@@ -475,13 +497,12 @@
             own[n] += rf[pl.ds(n * ROWS, ROWS), lanes(0)]
             xr[2 + n] = (xr[2 + n].astype(F32) + rf[pl.ds(n * ROWS, ROWS), lanes(1)]).astype(BF)
 
-    for n, ref in enumerate((att, dq, out_k, out_v)):
-        ref[:, lanes(1 - side)] = xr[n]
-    for n, ref in ((0, out_k), (1, out_v)):
-        ref[:, lanes(side)] = own[n].astype(BF)
+    out[:, :, lanes(1 - side)] = xr[...]
+    for n in range(2):
+        out[2 + n, :, lanes(side)] = own[n].astype(BF)
 
     for c in range(PAIRS):
-        for copy in cross(c) + x_back(c):
+        for copy in cross(1)[: 4 * c] + [x_back(c, n) for n in range(3)]:
             copy.wait_send()
         for copy in (to_near(c), to_far(c), near_back(c), far_back(c), swap(c)):
             copy.wait_send()
@@ -512,11 +533,11 @@
     hbm = pl.BlockSpec(memory_space=pl.ANY)
     dma = pltpu.SemaphoreType.DMA
     two = dma((PAIRS,))
-    return pl.pallas_call(
+    whole = pl.pallas_call(
         kernel,
-        out_shape=[jax.ShapeDtypeStruct((ROWS, WIDTH), BF)] * 4,
+        out_shape=jax.ShapeDtypeStruct((4, ROWS, WIDTH), BF),
         in_specs=[smem, smem, hbm, hbm, hbm, hbm],
-        out_specs=[vmem] * 4,
+        out_specs=vmem,
         scratch_shapes=[
             pltpu.VMEM((2, CAND, MINE), BF),
             pltpu.VMEM((2, 2 * ROWS, MINE), BF),
@@ -549,7 +570,7 @@
             pltpu.VMEM((2 * ROWS, WIDTH), F32),
             dma((4,)), dma, dma, dma((4 * PAIRS,)), dma((4 * PAIRS,)), two, two, two, two,
             dma, dma, dma, dma, dma, dma, dma, dma,
-            two, two, two, two, dma((2 * PAIRS,)), dma((2 * PAIRS,)),
+            two, two, two, two, dma((3 * PAIRS,)), dma((3 * PAIRS,)),
             two, two, two, two, two, two, two, two,
         ],
         compiler_params=pltpu.CompilerParams(
@@ -557,6 +578,7 @@
         ),
         name="banded",
     )(band, prefix_len, query, keys, values, grad_out)
+    return tuple(whole[n] for n in range(4))
 
 
 def solution(mesh):

time: 110 us -> 101 us (0.918)
  Pallas kernels: 103 us -> 96.2 us
  local copies, waits for them, and re-layouts: 5.18 us -> 2.86 us
    pallas_call x1, Pallas kernels: 103 us -> 96.2 us  [on_device(): pl.pallas_call(kernel, out_shape=jax.ShapeDtypeStruct((4, ROWS, WIDTH), B...]
    unnamed x10 -> x0, local copies, waits for them, and re-layouts: 5.18 us -> none
    squeeze x0 -> x1, local copies, waits for them, and re-layouts: none -> 2.86 us  [on_device(): return tuple((whole[n] for n in range(4)))]
where the time goes in v3:
time: 101 us; the launch traced here: 100 us
  Pallas kernels  96.2 us (95%)
  local copies, waits for them, and re-layouts  2.86 us (3%)
  between operations  1.29 us (1%)
    pallas_call x1, Pallas kernels, on_device(): pl.pallas_call(kernel, out_shape=jax.ShapeDtypeStruct((4, ROWS, WIDTH), B...  96.2 us
    squeeze x1, local copies, waits for them, and re-layouts, on_device(): return tuple((whole[n] for n in range(4)))  2.86 us

profile of v3, /device:TPU:0, one launch (start us, length us, event | category | flops | bytes accessed | tf_op | source)
XLA Modules:
  0.0 100.4 jit_solution(15004698006410019548)
XLA Ops:
  1.3 96.2 %banded.1 = bf16[4,512,512]{2,1,0:T(8,128)(2,1)} custom-call(s32[2,5]{1,0:T(2,128)} %band.1, s32[1]{0:T(128)S(6)} %copy.10.plen, bf16[512,512]{1,0:T(8,128)(2,1)} %q.1, bf16[512,512]{1,0:T(8,128)(2,1)} %k.1, bf16[512,512]{1,0:T(8,128)(2,1)} %v.1, bf16[512,512]{1,0:T(8,128)(2,1)} %g.1), custom_call_target="tpu_custom_call" | custom-call | tf_op jit(solution)/shard_map/banded/pallas_call | solution.py:536
  97.5 2.9 %slice_bitcast_fusion = (bf16[512,512]{1,0:T(8,128)(2,1)}, bf16[512,512]{1,0:T(8,128)(2,1)}, bf16[512,512]{1,0:T(8,128)(2,1)}, bf16[512,512]{1,0:T(8,128)(2,1)}) fusion(bf16[4,512,512]{2,1,0:T(8,128)(2,1)} %banded.1), kind=kLoop, calls=%fused_computation | loop fusion | bytes 4194304 | tf_op jit(solution)/shard_map/squeeze | solution.py:581

commit v4 on v3

--- a/solution.py
+++ b/solution.py
@@ -53,7 +53,7 @@
             bias[i, low : low + BLK, :] = jnp.where(row + s * BLK < plen[0], 0.0, OFF)
 
 
-def attend(p, u, kv, qg, bias, kt, vt, gt, x, e, dk, dv, att_t, dq_t, result, midway):
+def attend(p, u, kv, qg, bias, kt, vt, gt, x, e, dk, dv, att_t, dq_t, result, midway, later):
     cols = pl.ds(pl.multiple_of(p * PAIR, PAIR), PAIR)
     lane = lax.broadcasted_iota(jnp.int32, (BLK, PAIR), 1)
     combos = [(qb, h) for qb in range(2) for h in range(2)]
@@ -131,8 +131,11 @@
     for qb in range(2):
         result[0, mine(qb), cols] = att_t[qb].T.astype(BF)
     midway()
-    for n in range(4):
-        on_band(n)
+    on_band(0)
+    on_band(1)
+    later()
+    on_band(2)
+    on_band(3)
     for qb in range(2):
         result[1, mine(qb), cols] = dq_t[qb].T.astype(BF)
 
@@ -290,8 +293,21 @@
 
     note = send(listed.at[side], listed.at[side], l_s, l_r, partner)
     note.start()
-    for c in cross(0):
-        c.start()
+    groups = [cross(0)[:2], cross(0)[2:], cross(1)[:2], cross(1)[2:]]
+
+    def launch(n):
+        for c in groups[n]:
+            c.start()
+
+    def sent(n):
+        for c in groups[n]:
+            c.wait_send()
+
+    def arrived(n):
+        for c in groups[n]:
+            c.wait_recv()
+
+    launch(0)
     to_near(0).start()
 
     @pl.when(jnp.logical_and(bottom, jnp.logical_not(first)))
@@ -306,6 +322,10 @@
 
     note.wait()
     fill_bias(listed, plen, bias, 2 * (device - side))
+    sent(0)
+    launch(1)
+    arrived(0)
+    to_far(0).start()
 
     @pl.when(jnp.logical_not(bottom))
     def _():
@@ -313,17 +333,18 @@
 
     for n in range(1, PLANE):
         send(piece(core, spot), piece(core, spot), b3_s, b3_r, in_plane(z, peer(n), side, core)).start()
-    for c, later in zip(cross(0), cross(1)):
-        c.wait_send()
-        later.start()
-    for c in cross(0):
-        c.wait_recv()
-    to_far(0).start()
+    sent(1)
+    launch(2)
     to_near(1).start()
     wait_bytes(kv.at[0, pl.ds(0, (PLANE - 1) * PIECE)], b3_r)
     whole = kv.at[core, pl.ds(PROMPT, ROWS)]
     prompt = send(whole, whole, b4_s, b4_r, other_core)
     prompt.start()
+    arrived(1)
+    sent(2)
+    launch(3)
+    arrived(2)
+    to_far(1).start()
     prompt.wait()
 
     def near_back(c):
@@ -366,7 +387,6 @@
 
     def hand_back(c):
         cols = columns(c)
-        reduce_plane(c)
         for n, grad, scale in ((0, dk, SCALE), (1, dv, 1.0)):
             far_s[n, :, cols] = (grad[near_back_rows[1], :] * scale).astype(BF)
         far_back(c).start()
@@ -437,6 +457,11 @@
             dv[...] = jnp.zeros_like(dv)
 
             to_far(p).wait_recv()
+
+            @pl.when(p == 1)
+            def _():
+                arrived(3)
+
             cols = columns(p)
             kt[...] = kv[0, :, cols].T
             vt[...] = kv[1, :, cols].T
@@ -445,19 +470,23 @@
         u = jnp.where(late == 0, side, 1 - side)
 
         def midway():
-            @pl.when(t == 0)
-            def _():
-                for c in cross(1):
-                    c.wait_recv()
-                to_far(1).start()
-
             for c in range(PAIRS):
 
                 @pl.when(t == 2 * c + 1)
                 def _(c=c):
                     hand_prompt(c)
 
-        attend(p, u, kv, qg, bias, kt, vt, gt, x, e, dk, dv, att_t, dq_t, result, midway)
+        def later():
+            @pl.when(t == 1)
+            def _():
+                reduce_plane(0)
+
+            @pl.when(t == 3)
+            def _():
+                reduce_plane(1)
+                reduce_root(0)
+
+        attend(p, u, kv, qg, bias, kt, vt, gt, x, e, dk, dv, att_t, dq_t, result, midway, later)
 
         @pl.when(late == 0)
         def _():
@@ -478,13 +507,12 @@
         def _():
             hand_back(1)
 
-    reduce_root(0)
-    settle(0)
     reduce_column(1)
+    reduce_root(1)
     for n in range(2):
         out[n, :, lanes(side)] = result[n, run(side), :]
+    settle(0)
     settle(1)
-    reduce_root(1)
     for c in range(PAIRS):
         for n in range(3):
             x_back(c, n).wait_recv()
@@ -502,7 +530,7 @@
         out[2 + n, :, lanes(side)] = own[n].astype(BF)
 
     for c in range(PAIRS):
-        for copy in cross(1)[: 4 * c] + [x_back(c, n) for n in range(3)]:
+        for copy in (groups[3] if c else []) + [x_back(c, n) for n in range(3)]:
             copy.wait_send()
         for copy in (to_near(c), to_far(c), near_back(c), far_back(c), swap(c)):
             copy.wait_send()

time: 101 us -> 95.9 us (0.950)
  Pallas kernels: 96.2 us -> 90.5 us
    pallas_call x1, Pallas kernels: 96.2 us -> 90.5 us  [on_device(): pl.pallas_call(kernel, out_shape=jax.ShapeDtypeStruct((4, ROWS, WIDTH), B...]
where the time goes in v4:
time: 95.9 us; the launch traced here: 94.6 us
  Pallas kernels  90.5 us (94%)
  local copies, waits for them, and re-layouts  2.86 us (3%)
  between operations  1.29 us (1%)
    pallas_call x1, Pallas kernels, on_device(): pl.pallas_call(kernel, out_shape=jax.ShapeDtypeStruct((4, ROWS, WIDTH), B...  90.5 us
    squeeze x1, local copies, waits for them, and re-layouts, on_device(): return tuple((whole[n] for n in range(4)))  2.86 us

profile of v4, /device:TPU:0, one launch (start us, length us, event | category | flops | bytes accessed | tf_op | source)
XLA Modules:
  0.0 94.6 jit_solution(14639176213629447479)
XLA Ops:
  1.3 90.5 %banded.1 = bf16[4,512,512]{2,1,0:T(8,128)(2,1)} custom-call(s32[2,5]{1,0:T(2,128)} %band.1, s32[1]{0:T(128)S(6)} %copy.10.plen, bf16[512,512]{1,0:T(8,128)(2,1)} %q.1, bf16[512,512]{1,0:T(8,128)(2,1)} %k.1, bf16[512,512]{1,0:T(8,128)(2,1)} %v.1, bf16[512,512]{1,0:T(8,128)(2,1)} %g.1), custom_call_target="tpu_custom_call" | custom-call | tf_op jit(solution)/shard_map/banded/pallas_call | solution.py:564
  91.7 2.9 %slice_bitcast_fusion = (bf16[512,512]{1,0:T(8,128)(2,1)}, bf16[512,512]{1,0:T(8,128)(2,1)}, bf16[512,512]{1,0:T(8,128)(2,1)}, bf16[512,512]{1,0:T(8,128)(2,1)}) fusion(bf16[4,512,512]{2,1,0:T(8,128)(2,1)} %banded.1), kind=kLoop, calls=%fused_computation | loop fusion | bytes 4194304 | tf_op jit(solution)/shard_map/squeeze | solution.py:609

commit v5 on v4

--- a/solution.py
+++ b/solution.py
@@ -133,11 +133,11 @@
     midway()
     on_band(0)
     on_band(1)
+    result[1, mine(0), cols] = dq_t[0].T.astype(BF)
     later()
     on_band(2)
     on_band(3)
-    for qb in range(2):
-        result[1, mine(qb), cols] = dq_t[qb].T.astype(BF)
+    result[1, mine(1), cols] = dq_t[1].T.astype(BF)
 
 
 def wait_bytes(ref, sem):
@@ -148,8 +148,8 @@
     band, plen, q, k, v, g, out,
     kv, qg, listed, bias, kt, vt, gt, x, e, dk, dv, att_t, dq_t, result,
     own, near_s, near_r, far_s, far_r, xo, xr, ps, pr, rb, ry, pz, rz, pf, rf,
-    local_sem, l_s, l_r, x_s, x_r, e_s, e_r, f_s, f_r,
-    b1_s, b1_r, b2_s, b2_r, b3_s, b3_r, b4_s, b4_r,
+    column_sem, local_sem, l_s, l_r, x_s, x_r, e_s, e_r, f_s, f_r,
+    stage, b0_s, b0_r, b1_s, b1_r, b2_s, b2_r, b3_s, b3_r, b4_s, b4_r,
     n_s, n_r, w_s, w_r, o_s, o_r, r1_s, r1_r, r2_s, r2_r, r3_s, r3_r, r4_s, r4_r,
 ):
     outer = lax.axis_index("outer")
@@ -171,6 +171,9 @@
     root = (0, 0)
     first = device == 0
     bottom = z == 0
+    head = jnp.logical_and(bottom, jnp.logical_and(x_lo == 0, side == 0))
+    rest = jnp.logical_and(bottom, jnp.logical_not(jnp.logical_and(x_lo == 0, side == 0)))
+    row = inner // 2
 
     def in_plane(level, at, part, which):
         return ((level * 2 + at % 2) * 2 + which, (at // 2) * 2 + part)
@@ -223,10 +226,6 @@
         def _(n):
             hello(in_column(n))
 
-    @pl.when(jnp.logical_not(bottom))
-    def _():
-        hello(in_column(0))
-
     def root_peer(n):
         return in_plane(0, n % PLANE, (n // PLANE) % 2, n // (2 * PLANE))
 
@@ -240,11 +239,20 @@
     def _():
         hello(root)
 
-    greeted = 4 + PLANE - 1 + jnp.where(bottom, 7, 1)
+    @pl.when(rest)
+    def _():
+        hello((core, 2 * row))
+
+    greeted = 4 + PLANE - 1 + jnp.where(bottom, 0, 1)
     greeted = greeted + jnp.where(first, 4 * PLANE - 1, jnp.where(bottom, 1, 0))
+    greeted = greeted + jnp.where(head, 3, 0)
     for c in mine_in:
         c.wait()
     pl.semaphore_wait(barrier, greeted)
+
+    @pl.when(jnp.logical_not(bottom))
+    def _():
+        pl.semaphore_signal(column_sem, inc=1, device_id=in_column(0), device_id_type=MESH)
 
     def send(src, dst, s_sem, r_sem, target):
         return pltpu.make_async_remote_copy(
@@ -275,21 +283,20 @@
     def piece(which, at):
         return kv.at[which, pl.ds(pl.multiple_of(PROMPT + at * PIECE, PIECE), PIECE)]
 
+    quarter = 2 * PIECE
+
     @pl.when(first)
     def _():
         for which, src, low in ((0, k, 1), (1, v, 0)):
 
-            @pl.loop(low, 2 * PLANE)
+            @pl.loop(low, 4)
             def _(n):
-                at = n % PLANE
-                send(
-                    src.at[strip(at), lanes(n // PLANE)], piece(which, at), b1_s, b1_r,
-                    root_peer(n + which * 2 * PLANE),
-                ).start()
-
-        own_piece = pltpu.make_async_copy(k.at[strip(0), lanes(0)], piece(0, 0), local_sem.at[0])
-        own_piece.start()
-        own_piece.wait()
+                part = src.at[pl.ds(pl.multiple_of(n * quarter, quarter), quarter)]
+                send(part, stage, b0_s, b0_r, (which, 2 * n)).start()
+
+        own_part = pltpu.make_async_copy(k.at[pl.ds(0, quarter)], stage, local_sem.at[0])
+        own_part.start()
+        own_part.wait()
 
     note = send(listed.at[side], listed.at[side], l_s, l_r, partner)
     note.start()
@@ -310,12 +317,30 @@
     launch(0)
     to_near(0).start()
 
-    @pl.when(jnp.logical_and(bottom, jnp.logical_not(first)))
+    @pl.when(jnp.logical_and(head, jnp.logical_not(first)))
+    def _():
+        wait_bytes(stage, b0_r)
+
+    @pl.when(head)
+    def _():
+        for n in range(1, 4):
+            src = stage.at[pl.ds((n % 2) * PIECE, PIECE), pl.ds((n // 2) * MINE, MINE)]
+            at = 2 * row + n % 2
+            send(src, piece(core, at), b1_s, b1_r, in_plane(0, at, n // 2, core)).start()
+        own_piece = pltpu.make_async_copy(
+            stage.at[pl.ds(0, PIECE), pl.ds(0, MINE)], piece(core, spot), local_sem.at[0]
+        )
+        own_piece.start()
+        own_piece.wait()
+
+    @pl.when(rest)
     def _():
         wait_bytes(piece(core, spot), b1_r)
 
     @pl.when(bottom)
     def _():
+        pl.semaphore_wait(column_sem, 7)
+
         @pl.loop(1, 8)
         def _(n):
             send(piece(core, spot), piece(core, spot), b2_s, b2_r, in_column(n)).start()
@@ -335,7 +360,6 @@
         send(piece(core, spot), piece(core, spot), b3_s, b3_r, in_plane(z, peer(n), side, core)).start()
     sent(1)
     launch(2)
-    to_near(1).start()
     wait_bytes(kv.at[0, pl.ds(0, (PLANE - 1) * PIECE)], b3_r)
     whole = kv.at[core, pl.ds(PROMPT, ROWS)]
     prompt = send(whole, whole, b4_s, b4_r, other_core)
@@ -346,6 +370,7 @@
     arrived(2)
     to_far(1).start()
     prompt.wait()
+    to_near(1).start()
 
     def near_back(c):
         return send(near_s.at[:, :, columns(c)], near_r.at[:, :, columns(c)], n_s.at[c], n_r.at[c], near)
@@ -354,11 +379,14 @@
         return send(far_s.at[:, :, columns(c)], far_r.at[:, :, columns(c)], w_s.at[c], w_r.at[c], far)
 
     def x_back(c, n):
-        if n < 2:
-            src, dst = result.at[n, run(1 - side), columns(c)], xr.at[n, :, columns(c)]
+        if n == 0:
+            src, dst = result.at[0, run(1 - side), columns(c)], xr.at[0, :, columns(c)]
+        elif n < 3:
+            rows = at_block((1 - side) * ROWS + (n - 1) * BLK)
+            src, dst = result.at[1, rows, columns(c)], xr.at[1, pl.ds((n - 1) * BLK, BLK), columns(c)]
         else:
             src, dst = xo.at[:, :, columns(c)], xr.at[2:4, :, columns(c)]
-        return send(src, dst, o_s.at[3 * c + n], o_r.at[3 * c + n], partner)
+        return send(src, dst, o_s.at[4 * c + n], o_r.at[4 * c + n], partner)
 
     def swap(c):
         return send(ps.at[1 - core, :, columns(c)], pr.at[:, columns(c)], r1_s.at[c], r1_r.at[c], other_core)
@@ -390,11 +418,13 @@
         for n, grad, scale in ((0, dk, SCALE), (1, dv, 1.0)):
             far_s[n, :, cols] = (grad[near_back_rows[1], :] * scale).astype(BF)
         far_back(c).start()
-        x_back(c, 1).start()
+        x_back(c, 2).start()
+        if c == 1:
+            reduce_column(c)
         near_back(c).wait_recv()
         for n, grad, scale in ((0, dk, SCALE), (1, dv, 1.0)):
             xo[n, :, cols] = (grad[run(2 - side), :] * scale + near_r[n, :, cols].astype(F32)).astype(BF)
-        x_back(c, 2).start()
+        x_back(c, 3).start()
         for n, grad, scale in ((0, dk, SCALE), (1, dv, 1.0)):
             own[n, :, cols] = grad[own_rows, :] * scale
 
@@ -480,10 +510,12 @@
             @pl.when(t == 1)
             def _():
                 reduce_plane(0)
+                x_back(0, 1).start()
 
             @pl.when(t == 3)
             def _():
                 reduce_plane(1)
+                x_back(1, 1).start()
                 reduce_root(0)
 
         attend(p, u, kv, qg, bias, kt, vt, gt, x, e, dk, dv, att_t, dq_t, result, midway, later)
@@ -507,14 +539,13 @@
         def _():
             hand_back(1)
 
-    reduce_column(1)
     reduce_root(1)
     for n in range(2):
         out[n, :, lanes(side)] = result[n, run(side), :]
     settle(0)
     settle(1)
     for c in range(PAIRS):
-        for n in range(3):
+        for n in range(4):
             x_back(c, n).wait_recv()
 
     @pl.when(first)
@@ -530,7 +561,7 @@
         out[2 + n, :, lanes(side)] = own[n].astype(BF)
 
     for c in range(PAIRS):
-        for copy in (groups[3] if c else []) + [x_back(c, n) for n in range(3)]:
+        for copy in (groups[3] if c else []) + [x_back(c, n) for n in range(4)]:
             copy.wait_send()
         for copy in (to_near(c), to_far(c), near_back(c), far_back(c), swap(c)):
             copy.wait_send()
@@ -550,9 +581,13 @@
     def _():
         wait_bytes(kv.at[0, pl.ds(0, 7 * PIECE)], b2_s)
 
+    @pl.when(head)
+    def _():
+        wait_bytes(kv.at[0, pl.ds(0, 3 * PIECE)], b1_s)
+
     @pl.when(first)
     def _():
-        wait_bytes(kv.at[0, pl.ds(0, (4 * PLANE - 1) * PIECE)], b1_s)
+        wait_bytes(kv.at[0, pl.ds(0, 7 * 2 * quarter)], b0_s)
 
 
 def on_device(query, keys, values, grad_out, band, prefix_len):
@@ -596,9 +631,11 @@
             pltpu.VMEM((8, PIECE, MINE), F32),
             pltpu.VMEM((PIECE, MINE), F32),
             pltpu.VMEM((2 * ROWS, WIDTH), F32),
+            pltpu.SemaphoreType.REGULAR,
             dma((4,)), dma, dma, dma((4 * PAIRS,)), dma((4 * PAIRS,)), two, two, two, two,
+            pltpu.VMEM((2 * PIECE, WIDTH), BF), dma, dma,
             dma, dma, dma, dma, dma, dma, dma, dma,
-            two, two, two, two, dma((3 * PAIRS,)), dma((3 * PAIRS,)),
+            two, two, two, two, dma((4 * PAIRS,)), dma((4 * PAIRS,)),
             two, two, two, two, two, two, two, two,
         ],
         compiler_params=pltpu.CompilerParams(

time: 95.9 us -> 94.2 us (0.982); the launches traced: 94.6 us -> 94 us
  no operation moved by 1% of the time
where the time goes in v5:
time: 94.2 us; the launch traced here: 94 us
  Pallas kernels  89.8 us (95%)
  local copies, waits for them, and re-layouts  2.86 us (3%)
  between operations  1.29 us (1%)
    pallas_call x1, Pallas kernels, on_device(): pl.pallas_call(kernel, out_shape=jax.ShapeDtypeStruct((4, ROWS, WIDTH), B...  89.8 us
    squeeze x1, local copies, waits for them, and re-layouts, on_device(): return tuple((whole[n] for n in range(4)))  2.86 us

profile of v5, /device:TPU:0, one launch (start us, length us, event | category | flops | bytes accessed | tf_op | source)
XLA Modules:
  0.0 94.0 jit_solution(4325940937634140377)
XLA Ops:
  1.3 89.8 %banded.1 = bf16[4,512,512]{2,1,0:T(8,128)(2,1)} custom-call(s32[2,5]{1,0:T(2,128)} %band.1, s32[1]{0:T(128)S(6)} %copy.10.plen, bf16[512,512]{1,0:T(8,128)(2,1)} %q.1, bf16[512,512]{1,0:T(8,128)(2,1)} %k.1, bf16[512,512]{1,0:T(8,128)(2,1)} %v.1, bf16[512,512]{1,0:T(8,128)(2,1)} %g.1), custom_call_target="tpu_custom_call" | custom-call | tf_op jit(solution)/shard_map/banded/pallas_call | solution.py:599
  91.1 2.9 %slice_bitcast_fusion = (bf16[512,512]{1,0:T(8,128)(2,1)}, bf16[512,512]{1,0:T(8,128)(2,1)}, bf16[512,512]{1,0:T(8,128)(2,1)}, bf16[512,512]{1,0:T(8,128)(2,1)}) fusion(bf16[4,512,512]{2,1,0:T(8,128)(2,1)} %banded.1), kind=kLoop, calls=%fused_computation | loop fusion | bytes 4194304 | tf_op jit(solution)/shard_map/squeeze | solution.py:646

commit v6 on v5

--- a/solution.py
+++ b/solution.py
@@ -365,11 +365,11 @@
     prompt = send(whole, whole, b4_s, b4_r, other_core)
     prompt.start()
     arrived(1)
-    sent(2)
-    launch(3)
     arrived(2)
     to_far(1).start()
     prompt.wait()
+    sent(2)
+    launch(3)
     to_near(1).start()
 
     def near_back(c):

time: 94.2 us -> 94.9 us (level); the launches traced: 94 us -> 93.6 us
  no operation moved by 1% of the time
where the time goes in v6:
time: 94.9 us; the launch traced here: 93.6 us
  Pallas kernels  89.5 us (94%)
  local copies, waits for them, and re-layouts  2.86 us (3%)
  between operations  1.29 us (1%)
    pallas_call x1, Pallas kernels, on_device(): pl.pallas_call(kernel, out_shape=jax.ShapeDtypeStruct((4, ROWS, WIDTH), B...  89.5 us
    squeeze x1, local copies, waits for them, and re-layouts, on_device(): return tuple((whole[n] for n in range(4)))  2.86 us

profile of v6, /device:TPU:0, one launch (start us, length us, event | category | flops | bytes accessed | tf_op | source)
XLA Modules:
  0.0 93.6 jit_solution(18238270620385142546)
XLA Ops:
  1.3 89.5 %banded.1 = bf16[4,512,512]{2,1,0:T(8,128)(2,1)} custom-call(s32[2,5]{1,0:T(2,128)} %band.1, s32[1]{0:T(128)S(6)} %copy.10.plen, bf16[512,512]{1,0:T(8,128)(2,1)} %q.1, bf16[512,512]{1,0:T(8,128)(2,1)} %k.1, bf16[512,512]{1,0:T(8,128)(2,1)} %v.1, bf16[512,512]{1,0:T(8,128)(2,1)} %g.1), custom_call_target="tpu_custom_call" | custom-call | tf_op jit(solution)/shard_map/banded/pallas_call | solution.py:599
  90.7 2.9 %slice_bitcast_fusion = (bf16[512,512]{1,0:T(8,128)(2,1)}, bf16[512,512]{1,0:T(8,128)(2,1)}, bf16[512,512]{1,0:T(8,128)(2,1)}, bf16[512,512]{1,0:T(8,128)(2,1)}) fusion(bf16[4,512,512]{2,1,0:T(8,128)(2,1)} %banded.1), kind=kLoop, calls=%fused_computation | loop fusion | bytes 4194304 | tf_op jit(solution)/shard_map/squeeze | solution.py:646
